TPU v7x, 32 devices: a whole 2x2x4 slice. The times are simulated.
32 devices in a mesh: groups: 2 (over y), span: 2 (over x), tok: 4 (over z), head: 2 (over core).
Axes of the slice: x: 2, y: 2, z: 4, core: 2. Of those that a mesh axis runs over, the one named last changes fastest.
Arguments:
- queries: bfloat16 [16384, 2, 256], P(('groups', 'span', 'tok'), 'head'), parts along dimension 0, may hold values from -6 to 6
- keys: bfloat16 [16384, 2, 256], P(('groups', 'span', 'tok'), 'head'), parts along dimension 0, may hold values from -6 to 6
- values: bfloat16 [16384, 2, 256], P(('groups', 'span', 'tok'), 'head'), parts along dimension 0, may hold values from -6 to 6
- rates: float32 [16384, 2], P(('groups', 'span', 'tok'), 'head'), parts along dimension 0, may hold values from 0.0001 to 0.001
- w_in: bfloat16 [2, 2, 256, 256], P('head'), may hold values from -0.375 to 0.375
- w_out: bfloat16 [2, 256, 256], P('head'), may hold values from -0.375 to 0.375
- gain: float32 [2, 256], P('head'), may hold values from 0.1 to 1.9
- block_doc: int32 [128], P('groups'), parts along dimension 0, may hold values from 0 to 15, never falling along the last dimension, each value on 1 to 8 neighbouring positions
Outputs:
- mixed: bfloat16 [16384, 2, 256], P(('groups', 'span', 'tok'), 'head'), parts along dimension 0
There are 2 independent parts, one for each index of `groups`. A program takes and returns all parts, laid end to end along the dimension named above; an argument that names none is the same for every part. Nothing has to cross between parts.
Inputs may be any that keep to these rules, and one draw needn't show every extreme that they name: block_doc never falls from one block to the next; each document covers 1 to 8 consecutive blocks, one exactly 8.
All inputs are finite; a program needn't handle non-finite values.
Results may differ from a plain program's by a relative error of at most 0.01.
Values may be sent and summed in bfloat16 or wider, within the bound.
A program may use at most 64 MiB of HBM per device.

v0:
```python
import math
import jax
import jax.numpy as jnp
from jax import lax
from jax.sharding import PartitionSpec as P

BLOCK = 128
EPSILON = 1e-06


def from_behind(block, axis, distance):
    devices = range(lax.axis_size(axis))
    route = [(i - distance, i) for i in devices if i - distance in devices]
    return lax.ppermute(block, axis, route)


def rms_scale(inputs):
    return inputs * lax.rsqrt(jnp.mean(inputs * inputs, axis=-1, keepdims=True) + EPSILON)


def silu_slope(pre):
    sigmoid_val = jax.nn.sigmoid(pre)
    return sigmoid_val * (1.0 + pre * (1.0 - sigmoid_val))


def renormalize(updated, row_norm):
    scale = row_norm * lax.rsqrt(jnp.sum(updated * updated, axis=-1, keepdims=True) + EPSILON)
    return (updated * scale).astype(jnp.bfloat16)


def local_gradient(keys_norm, values, rates, w_in, w_out):
    gate_pre = jnp.einsum("thd,hfd->thf", keys_norm, w_in[:, 0], preferred_element_type=jnp.float32)
    up_pre = jnp.einsum("thd,hfd->thf", keys_norm, w_in[:, 1], preferred_element_type=jnp.float32)
    activation = (jax.nn.silu(gate_pre) * up_pre).astype(jnp.bfloat16)
    target = (-(rates[:, :, None] * values.astype(jnp.float32))).astype(jnp.bfloat16)
    act_grad = jnp.einsum("thd,hdf->thf", target, w_out, preferred_element_type=jnp.float32)
    gate_grad = (act_grad * up_pre * silu_slope(gate_pre)).astype(jnp.bfloat16)
    up_grad = (act_grad * jax.nn.silu(gate_pre)).astype(jnp.bfloat16)
    stacked = jnp.stack([gate_grad, up_grad], axis=1)
    grad_in = jnp.einsum("tchf,thd->hcfd", stacked, keys_norm, preferred_element_type=jnp.float32)
    grad_out = jnp.einsum("thd,thf->hdf", target, activation, preferred_element_type=jnp.float32)
    return (grad_in, grad_out)


def attend_blocks(query_norm, keys_norm, values, prior_keys, prior_values, prior_open):
    tokens, heads, width = query_norm.shape
    block_count = tokens // BLOCK
    shape = (block_count, BLOCK, heads, width)
    window_keys = jnp.concatenate([prior_keys.reshape(shape), keys_norm.reshape(shape)], axis=1)
    window_values = jnp.concatenate([prior_values.reshape(shape), values.reshape(shape)], axis=1)
    scores = jnp.einsum(
        "nqhd,nkhd->nhqk",
        query_norm.reshape(shape),
        window_keys,
        preferred_element_type=jnp.float32,
    ) / math.sqrt(width)
    row_pos = lax.broadcasted_iota(jnp.int32, (BLOCK, 2 * BLOCK), 0)
    col_pos = lax.broadcasted_iota(jnp.int32, (BLOCK, 2 * BLOCK), 1)
    inside = col_pos - BLOCK <= row_pos
    visible = jnp.where(col_pos[None] < BLOCK, prior_open[:, None, None], inside[None])
    weights = jnp.where(visible[:, None], jnp.exp(scores), 0.0)
    probabilities = (weights / jnp.sum(weights, axis=-1, keepdims=True)).astype(jnp.bfloat16)
    attended = jnp.einsum(
        "nhqk,nkhd->nqhd", probabilities, window_values, preferred_element_type=jnp.float32
    )
    return attended.reshape(tokens, heads, width)


def body(queries, keys, values, rates, w_in, w_out, gain, block_doc):
    query_norm = rms_scale(queries.astype(jnp.float32)).astype(jnp.bfloat16)
    keys_norm = rms_scale(keys.astype(jnp.float32)).astype(jnp.bfloat16)
    span_pos = lax.axis_index("span")
    span_count = lax.axis_size("span")
    tok_pos = lax.axis_index("tok")
    tok_count = lax.axis_size("tok")
    norm_in = jnp.sqrt(jnp.sum(jnp.square(w_in.astype(jnp.float32)), axis=-1, keepdims=True))
    norm_out = jnp.sqrt(jnp.sum(jnp.square(w_out.astype(jnp.float32)), axis=-1, keepdims=True))
    zeros_in = jnp.zeros(w_in.shape, jnp.float32)
    zeros_out = jnp.zeros(w_out.shape, jnp.float32)
    hidden_rows = w_in.shape[2] // tok_count
    feature_rows = w_out.shape[1] // tok_count

    def shard_of(full_in, full_out):
        return (
            lax.dynamic_slice_in_dim(full_in, tok_pos * hidden_rows, hidden_rows, 2),
            lax.dynamic_slice_in_dim(full_out, tok_pos * feature_rows, feature_rows, 1),
        )

    part_norm_in, part_norm_out = shard_of(norm_in, norm_out)

    def gradient_at(link_step, full_in, full_out):
        return lax.cond(
            span_pos == link_step,
            lambda: local_gradient(keys_norm, values, rates, full_in, full_out),
            lambda: (zeros_in, zeros_out),
        )

    def advance(link_step, state_carry):
        full_in, full_out, own_in, own_out = state_carry
        grad_in, grad_out = gradient_at(link_step, full_in, full_out)
        sum_in, sum_out = (
            lax.psum_scatter(
                grad_in.astype(jnp.bfloat16), "tok", scatter_dimension=2, tiled=True
            ).astype(jnp.float32),
            lax.psum_scatter(
                grad_out.astype(jnp.bfloat16), "tok", scatter_dimension=1, tiled=True
            ).astype(jnp.float32),
        )
        new_in = renormalize(own_in.astype(jnp.float32) - sum_in, part_norm_in)
        new_out = renormalize(own_out.astype(jnp.float32) - sum_out, part_norm_out)
        got_in, got_out = from_behind((new_in, new_out), "span", 1)
        receiver = span_pos == link_step + 1
        own_in = jnp.where(receiver, got_in, own_in)
        own_out = jnp.where(receiver, got_out, own_out)
        full_in, full_out = (
            lax.all_gather(own_in, "tok", axis=2, tiled=True),
            lax.all_gather(own_out, "tok", axis=1, tiled=True),
        )
        return (full_in, full_out, own_in, own_out)

    start_in, start_out = shard_of(w_in, w_out)
    fast_in, fast_out_w, last_in, last_out = lax.fori_loop(
        0, span_count - 1, advance, (w_in, w_out, start_in, start_out)
    )
    gate_pre = jnp.einsum(
        "thd,hfd->thf", query_norm, fast_in[:, 0], preferred_element_type=jnp.float32
    )
    up_pre = jnp.einsum(
        "thd,hfd->thf", query_norm, fast_in[:, 1], preferred_element_type=jnp.float32
    )
    activation = (jax.nn.silu(gate_pre) * up_pre).astype(jnp.bfloat16)
    fast_output = jnp.einsum(
        "thf,hdf->thd", activation, fast_out_w, preferred_element_type=jnp.float32
    )
    ttt = rms_scale(fast_output) * gain[None]
    before_keys, before_values = from_behind(
        (keys_norm[-BLOCK:], values[-BLOCK:]), ("span", "tok"), 1
    )
    prior_keys = jnp.concatenate([before_keys, keys_norm[:-BLOCK]], axis=0)
    prior_values = jnp.concatenate([before_values, values[:-BLOCK]], axis=0)
    block_count = queries.shape[0] // BLOCK
    device_index = span_pos * tok_count + tok_pos
    padded_docs = jnp.concatenate([jnp.full((1,), -1, jnp.int32), block_doc])
    block_start = device_index * block_count
    prior_docs = lax.dynamic_slice_in_dim(padded_docs, block_start, block_count)
    own_docs = lax.dynamic_slice_in_dim(padded_docs, block_start + 1, block_count)
    prior_open = prior_docs == own_docs
    attended = attend_blocks(query_norm, keys_norm, values, prior_keys, prior_values, prior_open)
    return (attended + ttt).astype(jnp.bfloat16)


def solution(mesh):
    placed = (
        P(("groups", "span", "tok"), "head", None),
        P(("groups", "span", "tok"), "head", None),
        P(("groups", "span", "tok"), "head", None),
        P(("groups", "span", "tok"), "head"),
        P("head", None, None, None),
        P("head", None, None),
        P("head", None),
        P("groups"),
    )
    return jax.shard_map(
        body,
        mesh=mesh,
        in_specs=placed,
        out_specs=P(("groups", "span", "tok"), "head", None),
        check_vma=False,
    )
```

profile of v0, /device:TPU:0, one launch (start us, length us, event | category | flops | bytes accessed | tf_op | source)
XLA Modules:
  0.0 98.3 jit_solution(1689548513804843051)
XLA Ops:
  6.5 0.0 reduce-scatter.3.cloned.1.call-start
  6.6 1.3 %fusion.28 = f32[1024]{0:T(1024)S(1)} fusion(bf16[1024,1,256]{2,0,1:T(8,128)(2,1)} %param.11), kind=kLoop, calls=%fused_computation.43 | loop fusion | flops 785408 | bytes 528384 | tf_op jit(solution)/shard_map/reduce_sum | solution.py:18
  7.9 1.2 %fusion.29 = bf16[1024,1,256]{2,0,1:T(8,128)(2,1)S(1)} fusion(bf16[1024,1,256]{2,0,1:T(8,128)(2,1)} %param.11, f32[1024]{0:T(1024)S(1)} %add_rsqrt_fusion.1), kind=kLoop, calls=%fused_computation.44 | loop fusion | flops 786432 | bytes 1052672 | tf_op jit(solution)/shard_map/convert_element_type | solution.py:71
  9.2 2.6 %conditional.1 = (bf16[1,2,256,256]{3,2,1,0:T(8,128)(2,1)S(1)}, bf16[1,256,256]{2,1,0:T(8,128)(2,1)S(1)}) conditional(s32[]{:T(128)} %convert_element_type.85, () %tuple.15, (f32[1024,1]{0,1:T(1,128)S(1)}, bf16[1024,1,256]{2,0,1:T(8,128)(2,1)S(1)}, bf16[1,256,256]{2,1,0:T(8,128)(2,1)S(1)}, bf16[1,2,256,256]{3,2,1,0:T(8,128)(2,1)S(1)}, ...), branch_computations={%region_3.0_spmd, %region_4.5_spmd} | conditional | flops 812908544 | bytes 11804688 | solution.py:92
  9.2 0.3 convolution_bitcast_fusion
  9.6 0.3 convolution_bitcast_fusion.1
  9.9 0.7 fusion.10
  10.6 0.5 convolution_bitcast_fusion.3
  11.1 0.6 convolution_bitcast_fusion.4
  11.8 0.0 copy-start.2
  11.8 0.6 copy-done.5
  12.4 0.0 reduce-scatter.3.cloned.1.call-update
  12.5 0.0 reduce-scatter.5.cloned.1.call-start
  12.5 4.9 %collective-permute-start.1 = (bf16[128,1,256]{2,0,1:T(8,128)(2,1)S(1)}, bf16[128,1,256]{2,0,1:T(8,128)(2,1)S(1)}, u32[]{:S(2)}, u32[]{:S(2)}) collective-permute-start(bf16[128,1,256]{2,0,1:T(8,128)(2,1)S(1)} %slice.30), channel_id=1, source_target_pairs={{0,2},{2,4},{4,6},{6,8},{8,10},{10,12},{12,14},{1,3},{3,5},{5,7},{... | collective-permute-start | bytes 196616 | tf_op jit(solution)/shard_map/ppermute | solution.py:14
  17.5 3.5 %collective-permute-start = (bf16[128,1,256]{2,0,1:T(8,128)(2,1)S(1)}, bf16[128,1,256]{2,0,1:T(8,128)(2,1)S(1)}, u32[]{:S(2)}, u32[]{:S(2)}) collective-permute-start(bf16[128,1,256]{2,0,1:T(8,128)(2,1)S(1)} %slice.24), channel_id=1, source_target_pairs={{0,2},{2,4},{4,6},{6,8},{8,10},{10,12},{12,14},{1,3},{3,5},{5,7},{... | collective-permute-start | bytes 196616 | tf_op jit(solution)/shard_map/ppermute | solution.py:14
  21.0 0.0 reduce-scatter.5.cloned.1.call-update
  21.0 0.1 multiply_reduce_fusion.1
  21.2 0.0 copy-start
  21.2 0.1 multiply_reduce_fusion.2
  21.4 0.0 copy-start.10
  21.4 0.8 copy-done
  22.2 0.2 fusion.26
  22.4 0.2 fusion.27
  22.7 0.1 pad_add_fusion
  22.8 0.1 dynamic-slice_compare_fusion
  22.9 0.0 collective-permute-done.1
  22.9 1.5 %fusion.23 = f32[8,128,256]{2,1,0:T(8,128)} fusion(bf16[8,128,256]{2,1,0:T(8,128)(2,1)S(1)} %bitcast.130, bf16[8,128,1,256]{3,1,0,2:T(8,128)(2,1)S(1)} %bitcast.129, bf16[8,128,1,256]{3,1,0,2:T(8,128)(2,1)S(1)} %bitcast.133, pred[128,256]{1,0:T(8,128)(4,1)S(1)} %get-tuple-element.71, pred[128,256]{1,0:T(8,128)(4,1)S(1)} %get-tuple-element.72, ...), kind=kOutput, calls=%fused_computation.34 | convolution fusion | flops 137101312 | bytes 2686984 | tf_op jit(solution)/shard_map/nqhd,nkhd->nhqk/dot_general | solution.py:51
  24.5 1.0 %copy-done.4 = bf16[1024,1,256]{2,0,1:T(8,128)(2,1)S(1)} copy-done((bf16[1024,1,256]{2,0,1:T(8,128)(2,1)S(1)}, bf16[1024,1,256]{2,0,1:T(8,128)(2,1)}, u32[]{:S(2)}) %copy-start.4) | copy-done | bytes 524312
  25.5 1.9 %fusion.32 = f32[8,256,128]{1,2,0:T(8,128)S(1)} fusion(bf16[8,128,1,256]{3,1,0,2:T(8,128)(2,1)S(1)} %bitcast.132, bf16[8,128,1,256]{3,1,0,2:T(8,128)(2,1)S(1)} %bitcast.134, f32[8,128,256]{2,1,0:T(8,128)} %fusion.23), kind=kOutput, calls=%fused_computation.49 | convolution fusion | flops 136840448 | bytes 3145728 | tf_op jit(solution)/shard_map/nhqk,nkhd->nqhd/dot_general | solution.py:63
  27.4 0.3 copy.19
  27.7 5.8 %reduce-scatter.3.cloned.1.call-done = bf16[1,64,256]{2,1,0:T(8,128)(2,1)} async-done(((bf16[1,256,256]{2,1,0:T(8,128)(2,1)}), bf16[1,64,256]{2,1,0:T(8,128)(2,1)}) %reduce-scatter.3.cloned.1.call-update) | async-done | bytes 32784 | tf_op jit(solution)/shard_map/while/body/eval_jaxpr/reduce_scatter | solution.py:105
  33.6 0.9 multiply_reduce_fusion.4
  34.5 0.1 rsqrt_multiply_fusion
  34.5 0.8 multiply_convert_fusion.4
  35.4 3.3 %collective-permute-start.2 = (bf16[1,64,256]{2,1,0:T(8,128)(2,1)S(1)}, bf16[1,64,256]{2,1,0:T(8,128)(2,1)S(1)}, u32[]{:S(2)}, u32[]{:S(2)}) collective-permute-start(bf16[1,64,256]{2,1,0:T(8,128)(2,1)S(1)} %multiply_convert_fusion.4), channel_id=1, source_target_pairs={{0,8},{1,9},{2,10},{3,11},{4,12},{5,13},{6,14},{7,15},{16,24},{17,... | collective-permute-start | bytes 98312 | tf_op jit(solution)/shard_map/while/body/eval_jaxpr/ppermute | solution.py:14
  38.7 14.9 %reduce-scatter.5.cloned.1.call-done = bf16[1,2,64,256]{3,2,1,0:T(8,128)(2,1)} async-done(((bf16[1,2,256,256]{3,2,1,0:T(8,128)(2,1)}), bf16[1,2,64,256]{3,2,1,0:T(8,128)(2,1)}) %reduce-scatter.5.cloned.1.call-update) | async-done | bytes 65552 | tf_op jit(solution)/shard_map/while/body/eval_jaxpr/reduce_scatter | solution.py:102
  53.6 0.9 multiply_reduce_fusion.3
  54.6 0.1 fusion.44
  54.6 0.9 multiply_convert_fusion.3
  55.6 3.5 %collective-permute-start.3 = (bf16[1,2,64,256]{3,2,1,0:T(8,128)(2,1)S(1)}, bf16[1,2,64,256]{3,2,1,0:T(8,128)(2,1)S(1)}, u32[]{:S(2)}, u32[]{:S(2)}) collective-permute-start(bf16[1,2,64,256]{3,2,1,0:T(8,128)(2,1)S(1)} %multiply_convert_fusion.3), channel_id=1, source_target_pairs={{0,8},{1,9},{2,10},{3,11},{4,12},{5,13},{6,14},{7,15},{16,24},{17,... | collective-permute-start | bytes 196616 | tf_op jit(solution)/shard_map/while/body/eval_jaxpr/ppermute | solution.py:14
  59.1 0.0 collective-permute-done.2
  59.1 13.5 %all_gather.8 = bf16[1,256,256]{2,1,0:T(8,128)(2,1)S(1)} all-gather(bf16[1,64,256]{2,1,0:T(8,128)(2,1)S(1)} %broadcast_select_fusion.1), channel_id=1, replica_groups=mesh['groups'=2,'span'=2,'tok'=4,'head'=2] {'tok'}, dimensions={1}, use_global_device_ids=true | all-gather | bytes 163840 | tf_op jit(solution)/shard_map/while/body/eval_jaxpr/all_gather | solution.py:117
  72.6 0.0 collective-permute-done.3
  72.6 14.4 %all_gather.9 = bf16[1,2,256,256]{3,2,1,0:T(8,128)(2,1)S(1)} all-gather(bf16[1,2,64,256]{3,2,1,0:T(8,128)(2,1)S(1)} %broadcast_select_fusion), channel_id=1, replica_groups=mesh['groups'=2,'span'=2,'tok'=4,'head'=2] {'tok'}, dimensions={2}, use_global_device_ids=true | all-gather | bytes 327680 | tf_op jit(solution)/shard_map/while/body/eval_jaxpr/all_gather | solution.py:116
  87.0 1.3 %convolution_bitcast_fusion.7 = f32[1024,1,256]{0,2,1:T(8,128)} fusion(bf16[1024,1,256]{2,0,1:T(8,128)(2,1)S(1)} %fusion.27, bf16[1,2,256,256]{3,2,1,0:T(8,128)(2,1)S(1)} %all_gather.9), kind=kOutput, calls=%fused_computation.31 | convolution fusion | flops 134217728 | bytes 1703936 | tf_op jit(solution)/shard_map/thd,hfd->thf/dot_general | solution.py:125
  88.4 1.9 %multiply_reduce_fusion = (f32[1024]{0:T(1024)S(1)}, f32[1,256,1024]{2,1,0:T(8,128)S(1)}) fusion(f32[1024,1,256]{0,2,1:T(8,128)} %convolution_bitcast_fusion.7, bf16[1024,1,256]{2,0,1:T(8,128)(2,1)S(1)} %fusion.27, bf16[1,2,256,256]{3,2,1,0:T(8,128)(2,1)S(1)} %all_gather.9, bf16[1,256,256]{2,1,0:T(8,128)(2,1)S(1)} %all_gather.8), kind=kOutput, calls=%fused_computation.54 | convolution fusion | flops 270531584 | bytes 2887680 | tf_op jit(solution)/shard_map/thf,hdf->thd/dot_general | solution.py:132
  90.3 0.2 fusion.35
  90.5 1.0 %copy.20 = bf16[1024,1,256]{2,0,1:T(8,128)(2,1)} copy(bf16[1024,1,256]{0,2,1:T(8,128)(2,1)S(1)} %fusion.35) | data formatting | bytes 1048576 | tf_op jit(solution)/shard_map/convert_element_type | solution.py:149
  (31 shorter events, 0.3 us)
Async XLA Ops:
  6.5 2.7 %copy-start.3 = (bf16[1024,1,256]{2,0,1:T(8,128)(2,1)S(1)}, bf16[1024,1,256]{2,0,1:T(8,128)(2,1)}, u32[]{:S(2)}) copy-start(bf16[1024,1,256]{2,0,1:T(8,128)(2,1)} %param.12) | copy-start | bytes 1572868
  6.5 2.7 %copy-start.9 = (f32[1024,1]{0,1:T(1,128)S(1)}, f32[1024,1]{0,1:T(1,128)}, u32[]{:S(2)}) copy-start(f32[1024,1]{0,1:T(1,128)} %param.13) | copy-start | bytes 12292
  6.5 2.7 %copy-start.1 = (bf16[1,2,256,256]{3,2,1,0:T(8,128)(2,1)S(1)}, bf16[1,2,256,256]{3,2,1,0:T(8,128)(2,1)}, u32[]{:S(2)}) copy-start(bf16[1,2,256,256]{3,2,1,0:T(8,128)(2,1)} %param.14) | copy-start | bytes 786436
  6.5 2.7 %copy-start.6 = (bf16[1,256,256]{2,1,0:T(8,128)(2,1)S(1)}, bf16[1,256,256]{2,1,0:T(8,128)(2,1)}, u32[]{:S(2)}) copy-start(bf16[1,256,256]{2,1,0:T(8,128)(2,1)} %param.15) | copy-start | bytes 393220
  6.5 27.0 %reduce-scatter.3.cloned.1.call-start = ((), (), s32[]{:S(2)}) async-start(), calls=%async_computation.2 | async-start | bytes 163840 | tf_op jit(solution)/shard_map/while/body/eval_jaxpr/reduce_scatter | solution.py:105
  11.8 0.6 copy-start.5
  11.8 9.2 %copy-start.2 = (bf16[1,2,256,256]{3,2,1,0:T(8,128)(2,1)}, bf16[1,2,256,256]{3,2,1,0:T(8,128)(2,1)S(1)}, u32[]{:S(2)}) copy-start(bf16[1,2,256,256]{3,2,1,0:T(8,128)(2,1)S(1)} %get-tuple-element.45) | copy-start | bytes 786436
  12.5 41.1 %reduce-scatter.5.cloned.1.call-start = ((), (), s32[]{:S(2)}) async-start(), calls=%async_computation.3 | async-start | bytes 327680 | tf_op jit(solution)/shard_map/while/body/eval_jaxpr/reduce_scatter | solution.py:102
  12.5 10.3 %collective-permute-start.1 = (bf16[128,1,256]{2,0,1:T(8,128)(2,1)S(1)}, bf16[128,1,256]{2,0,1:T(8,128)(2,1)S(1)}, u32[]{:S(2)}, u32[]{:S(2)}) collective-permute-start(bf16[128,1,256]{2,0,1:T(8,128)(2,1)S(1)} %slice.30), channel_id=1, source_target_pairs={{0,2},{2,4},{4,6},{6,8},{8,10},{10,12},{12,14},{1,3},{3,5},{5,7},{... | collective-permute-start | bytes 196616 | tf_op jit(solution)/shard_map/ppermute | solution.py:14
  17.5 6.9 %collective-permute-start = (bf16[128,1,256]{2,0,1:T(8,128)(2,1)S(1)}, bf16[128,1,256]{2,0,1:T(8,128)(2,1)S(1)}, u32[]{:S(2)}, u32[]{:S(2)}) collective-permute-start(bf16[128,1,256]{2,0,1:T(8,128)(2,1)S(1)} %slice.24), channel_id=1, source_target_pairs={{0,2},{2,4},{4,6},{6,8},{8,10},{10,12},{12,14},{1,3},{3,5},{5,7},{... | collective-permute-start | bytes 196616 | tf_op jit(solution)/shard_map/ppermute | solution.py:14
  21.2 1.0 %copy-start = (bf16[1024,1,256]{2,0,1:T(8,128)(2,1)S(1)}, bf16[1024,1,256]{2,0,1:T(8,128)(2,1)}, u32[]{:S(2)}) copy-start(bf16[1024,1,256]{2,0,1:T(8,128)(2,1)} %param.10) | copy-start | bytes 1572868
  21.4 1.3 %copy-start.10 = (s32[64]{0:T(128)S(1)}, s32[64]{0:T(128)}, u32[]{:S(2)}) copy-start(s32[64]{0:T(128)} %param.17) | copy-start | bytes 772
  24.4 1.0 %copy-start.4 = (bf16[1024,1,256]{2,0,1:T(8,128)(2,1)S(1)}, bf16[1024,1,256]{2,0,1:T(8,128)(2,1)}, u32[]{:S(2)}) copy-start(bf16[1024,1,256]{2,0,1:T(8,128)(2,1)} %param.12) | copy-start | bytes 1572868
  27.4 6.2 %copy-start.7 = (bf16[1,256,256]{2,1,0:T(8,128)(2,1)S(1)}, bf16[1,256,256]{2,1,0:T(8,128)(2,1)}, u32[]{:S(2)}) copy-start(bf16[1,256,256]{2,1,0:T(8,128)(2,1)} %param.15) | copy-start | bytes 393220
  35.4 23.7 %collective-permute-start.2 = (bf16[1,64,256]{2,1,0:T(8,128)(2,1)S(1)}, bf16[1,64,256]{2,1,0:T(8,128)(2,1)S(1)}, u32[]{:S(2)}, u32[]{:S(2)}) collective-permute-start(bf16[1,64,256]{2,1,0:T(8,128)(2,1)S(1)} %multiply_convert_fusion.4), channel_id=1, source_target_pairs={{0,8},{1,9},{2,10},{3,11},{4,12},{5,13},{6,14},{7,15},{16,24},{17,... | collective-permute-start | bytes 98312 | tf_op jit(solution)/shard_map/while/body/eval_jaxpr/ppermute | solution.py:14
  55.6 17.1 %collective-permute-start.3 = (bf16[1,2,64,256]{3,2,1,0:T(8,128)(2,1)S(1)}, bf16[1,2,64,256]{3,2,1,0:T(8,128)(2,1)S(1)}, u32[]{:S(2)}, u32[]{:S(2)}) collective-permute-start(bf16[1,2,64,256]{3,2,1,0:T(8,128)(2,1)S(1)} %multiply_convert_fusion.3), channel_id=1, source_target_pairs={{0,8},{1,9},{2,10},{3,11},{4,12},{5,13},{6,14},{7,15},{16,24},{17,... | collective-permute-start | bytes 196616 | tf_op jit(solution)/shard_map/while/body/eval_jaxpr/ppermute | solution.py:14
  88.4 1.9 %copy-start.8 = (f32[1,256]{1,0:T(1,128)S(1)}, f32[1,256]{1,0:T(1,128)}, u32[]{:S(2)}) copy-start(f32[1,256]{1,0:T(1,128)} %param.16) | copy-start | bytes 3076
Sparse Core Ops, SparseCore 0:
  12.6 20.9 reduce-scatter.2
  35.9 17.6 reduce-scatter.4
where the time goes:
time: 98.9 us; the launch traced here: 98.3 us
  blocking collectives  27.9 us (28%)
  waiting for transfers between devices  20.7 us (21%)
  starting transfers between devices  15.3 us (15%)
  between operations  13.8 us (14%)
  matrix products  9.19 us (9%)
  other arithmetic  7.46 us (8%)
  local copies, waits for them, and re-layouts  3.87 us (4%)
    ppermute x4, starting transfers between devices, from_behind(): return lax.ppermute(block, axis, route)  15.2 us
    reduce_scatter x1, waiting for transfers between devices, advance(): lax.psum_scatter(grad_in.astype(jnp.bfloat16), 'tok', scatter_dimension=2...  14.9 us
    all_gather x1, blocking collectives, advance(): lax.all_gather(own_in, 'tok', axis=2, tiled=True)  14.4 us
    all_gather x1, blocking collectives, advance(): lax.all_gather(own_out, 'tok', axis=1, tiled=True)  13.5 us
    reduce_scatter x1, waiting for transfers between devices, advance(): lax.psum_scatter(grad_out.astype(jnp.bfloat16), 'tok', scatter_dimension=...  5.84 us
    unnamed x22, local copies, waits for them, and re-layouts  2.46 us
  transfers between devices with their start and end apart: 6, of which 2 were waited for; matrix products, arithmetic and copies ran while one was open for 9% of the time, Pallas kernels for 0%

commit v1 on v0

--- a/solution.py
+++ b/solution.py
@@ -6,6 +6,27 @@
 
 BLOCK = 128
 EPSILON = 1e-06
+
+
+def gather_around(value, axis, dim):
+    size, index, extent = (lax.axis_size(axis), lax.axis_index(axis), value.shape[dim])
+    ahead = [(i, (i + 1) % size) for i in range(size)]
+    downward = [(i, (i - 1) % size) for i in range(size)]
+    out = jnp.zeros((*value.shape[:dim], size * extent, *value.shape[dim + 1 :]), value.dtype)
+    out = lax.dynamic_update_slice_in_dim(out, value, index * extent, axis=dim)
+    from_left = from_right = value
+    half = size // 2
+    for step in range(1, half + 1):
+        from_left = lax.ppermute(from_left, axis, ahead)
+        out = lax.dynamic_update_slice_in_dim(
+            out, from_left, (index - step) % size * extent, axis=dim
+        )
+        if step < size - half:
+            from_right = lax.ppermute(from_right, axis, downward)
+            out = lax.dynamic_update_slice_in_dim(
+                out, from_right, (index + step) % size * extent, axis=dim
+            )
+    return out
 
 
 def from_behind(block, axis, distance):
@@ -114,7 +135,7 @@
         own_out = jnp.where(receiver, got_out, own_out)
         full_in, full_out = (
             lax.all_gather(own_in, "tok", axis=2, tiled=True),
-            lax.all_gather(own_out, "tok", axis=1, tiled=True),
+            gather_around(own_out, "tok", 1),
         )
         return (full_in, full_out, own_in, own_out)
 

time: 98.9 us -> 86.9 us (0.88)
  blocking collectives: 27.9 us -> 13.9 us
  starting transfers between devices: 15.3 us -> 18.1 us
  waiting for transfers between devices: 20.7 us -> 18.9 us
    all_gather x1 -> x0, blocking collectives: 13.5 us -> none  [advance(): lax.all_gather(own_out, 'tok', axis=1, tiled=True)]
    reduce_scatter x1, waiting for transfers between devices: 14.9 us -> 5.2 us  [advance(): lax.psum_scatter(grad_in.astype(jnp.bfloat16), 'tok', scatter_dimension=2...]
    ppermute x4, waiting for transfers between devices: 0.01 us -> 3.39 us  [from_behind(): return lax.ppermute(block, axis, route)]
    reduce_scatter x1, waiting for transfers between devices: 5.84 us -> 9.15 us  [advance(): lax.psum_scatter(grad_out.astype(jnp.bfloat16), 'tok', scatter_dimension=...]
    ppermute x0 -> x3, starting transfers between devices: none -> 3.24 us  [the longest x1 3.24 us: gather_around(): from_right = lax.ppermute(from_right, axis, downward)]
    ppermute x0 -> x3, waiting for transfers between devices: none -> 1.12 us  [the longest x1 1.03 us: gather_around(): from_right = lax.ppermute(from_right, axis, downward)]
    unnamed x22 -> x24, local copies, waits for them, and re-layouts: 2.46 us -> 2.07 us
  transfers between devices with their start and end apart: 6 -> 9, of which waited for: 2 -> 6; matrix products, arithmetic and copies ran while one was open for 9% -> 12% of each run, Pallas kernels for 0% -> 0%
where the time goes in v1:
time: 86.9 us; the launch traced here: 86.2 us
  waiting for transfers between devices  18.9 us (22%)
  starting transfers between devices  18.1 us (21%)
  blocking collectives  13.9 us (16%)
  between operations  13.8 us (16%)
  matrix products  9.16 us (11%)
  other arithmetic  8.07 us (9%)
  local copies, waits for them, and re-layouts  4.3 us (5%)
    ppermute x4, starting transfers between devices, from_behind(): return lax.ppermute(block, axis, route)  14.7 us
    all_gather x1, blocking collectives, advance(): lax.all_gather(own_in, 'tok', axis=2, tiled=True)  13.9 us
    reduce_scatter x1, waiting for transfers between devices, advance(): lax.psum_scatter(grad_out.astype(jnp.bfloat16), 'tok', scatter_dimension=...  9.15 us
    reduce_scatter x1, waiting for transfers between devices, advance(): lax.psum_scatter(grad_in.astype(jnp.bfloat16), 'tok', scatter_dimension=2...  5.2 us
    ppermute x4, waiting for transfers between devices, from_behind(): return lax.ppermute(block, axis, route)  3.39 us
    ppermute x1, starting transfers between devices, gather_around(): from_right = lax.ppermute(from_right, axis, downward)  3.24 us
    unnamed x24, local copies, waits for them, and re-layouts  2.07 us
    dot_general x1, matrix products, attend_blocks(): jnp.einsum('nhqk,nkhd->nqhd', probabilities, window_values, preferred_ele...  1.94 us
  transfers between devices with their start and end apart: 9, of which 6 were waited for; matrix products, arithmetic and copies ran while one was open for 12% of the time, Pallas kernels for 0%

profile of v1, /device:TPU:0, one launch (start us, length us, event | category | flops | bytes accessed | tf_op | source)
XLA Modules:
  0.0 86.2 jit_solution(13657976858344189624)
XLA Ops:
  6.5 0.0 reduce-scatter.3.cloned.1.call-start
  6.6 1.3 %fusion.28 = f32[1024]{0:T(1024)S(1)} fusion(bf16[1024,1,256]{2,0,1:T(8,128)(2,1)} %param.11), kind=kLoop, calls=%fused_computation.43 | loop fusion | flops 785408 | bytes 528384 | tf_op jit(solution)/shard_map/reduce_sum | solution.py:39
  7.9 1.2 %fusion.29 = bf16[1024,1,256]{2,0,1:T(8,128)(2,1)S(1)} fusion(bf16[1024,1,256]{2,0,1:T(8,128)(2,1)} %param.11, f32[1024]{0:T(1024)S(1)} %add_rsqrt_fusion.1), kind=kLoop, calls=%fused_computation.44 | loop fusion | flops 786432 | bytes 1052672 | tf_op jit(solution)/shard_map/convert_element_type | solution.py:92
  9.2 2.6 %conditional.1 = (bf16[1,2,256,256]{3,2,1,0:T(8,128)(2,1)S(1)}, bf16[1,256,256]{2,1,0:T(8,128)(2,1)S(1)}) conditional(s32[]{:T(128)} %convert_element_type.85, () %tuple.15, (f32[1024,1]{0,1:T(1,128)S(1)}, bf16[1024,1,256]{2,0,1:T(8,128)(2,1)S(1)}, bf16[1,256,256]{2,1,0:T(8,128)(2,1)S(1)}, bf16[1,2,256,256]{3,2,1,0:T(8,128)(2,1)S(1)}, ...), branch_computations={%region_3.0_spmd, %region_4.5_spmd} | conditional | flops 812908544 | bytes 11804688 | solution.py:113
  9.2 0.3 convolution_bitcast_fusion
  9.6 0.3 convolution_bitcast_fusion.1
  9.9 0.7 fusion.10
  10.6 0.5 convolution_bitcast_fusion.3
  11.1 0.6 convolution_bitcast_fusion.4
  11.8 0.6 copy-done.5
  12.4 0.0 reduce-scatter.3.cloned.1.call-update
  12.5 0.0 reduce-scatter.5.cloned.1.call-start
  12.5 4.9 %collective-permute-start.1 = (bf16[128,1,256]{2,0,1:T(8,128)(2,1)S(1)}, bf16[128,1,256]{2,0,1:T(8,128)(2,1)S(1)}, u32[]{:S(2)}, u32[]{:S(2)}) collective-permute-start(bf16[128,1,256]{2,0,1:T(8,128)(2,1)S(1)} %slice.30), channel_id=1, source_target_pairs={{0,2},{2,4},{4,6},{6,8},{8,10},{10,12},{12,14},{1,3},{3,5},{5,7},{... | collective-permute-start | bytes 196616 | tf_op jit(solution)/shard_map/ppermute | solution.py:35
  17.5 3.5 %collective-permute-start = (bf16[128,1,256]{2,0,1:T(8,128)(2,1)S(1)}, bf16[128,1,256]{2,0,1:T(8,128)(2,1)S(1)}, u32[]{:S(2)}, u32[]{:S(2)}) collective-permute-start(bf16[128,1,256]{2,0,1:T(8,128)(2,1)S(1)} %slice.24), channel_id=1, source_target_pairs={{0,2},{2,4},{4,6},{6,8},{8,10},{10,12},{12,14},{1,3},{3,5},{5,7},{... | collective-permute-start | bytes 196616 | tf_op jit(solution)/shard_map/ppermute | solution.py:35
  21.0 0.0 reduce-scatter.5.cloned.1.call-update
  21.0 0.1 multiply_reduce_fusion.2
  21.2 0.1 multiply_reduce_fusion.1
  21.5 0.8 copy-done
  22.2 0.2 fusion.26
  22.5 0.2 fusion.27
  22.7 0.1 pad_add_fusion
  22.8 0.1 dynamic-slice_compare_fusion
  22.9 1.5 %fusion.23 = f32[8,128,256]{2,1,0:T(8,128)} fusion(bf16[8,128,256]{2,1,0:T(8,128)(2,1)S(1)} %bitcast.134, bf16[8,128,1,256]{3,1,0,2:T(8,128)(2,1)S(1)} %bitcast.133, bf16[8,128,1,256]{3,1,0,2:T(8,128)(2,1)S(1)} %bitcast.138, pred[128,256]{1,0:T(8,128)(4,1)S(1)} %get-tuple-element.73, pred[128,256]{1,0:T(8,128)(4,1)S(1)} %get-tuple-element.74, ...), kind=kOutput, calls=%fused_computation.34 | convolution fusion | flops 137101312 | bytes 2686984 | tf_op jit(solution)/shard_map/nqhd,nkhd->nhqk/dot_general | solution.py:72
  24.4 9.2 %reduce-scatter.3.cloned.1.call-done = bf16[1,64,256]{2,1,0:T(8,128)(2,1)} async-done(((bf16[1,256,256]{2,1,0:T(8,128)(2,1)}), bf16[1,64,256]{2,1,0:T(8,128)(2,1)}) %reduce-scatter.3.cloned.1.call-update) | async-done | bytes 32784 | tf_op jit(solution)/shard_map/while/body/eval_jaxpr/reduce_scatter | solution.py:126
  33.6 0.9 %multiply_reduce_fusion.4 = f32[64]{0:T(128)S(1)} fusion(bf16[1,64,256]{2,1,0:T(8,128)(2,1)} %reduce-scatter.3.cloned.1.call-done, bf16[1,256,256]{2,1,0:T(8,128)(2,1)S(1)} %copy-done.6, s32[]{:T(128)S(6)} %select_n.79), kind=kLoop, calls=%fused_computation.72 | loop fusion | flops 81856 | bytes 65796 | tf_op jit(solution)/shard_map/while/body/eval_jaxpr/reduce_sum | solution.py:48
  34.5 0.1 rsqrt_multiply_fusion
  34.5 0.8 multiply_convert_fusion.4
  35.4 3.3 %collective-permute-start.2 = (bf16[1,64,256]{2,1,0:T(8,128)(2,1)S(1)}, bf16[1,64,256]{2,1,0:T(8,128)(2,1)S(1)}, u32[]{:S(2)}, u32[]{:S(2)}) collective-permute-start(bf16[1,64,256]{2,1,0:T(8,128)(2,1)S(1)} %multiply_convert_fusion.4), channel_id=1, source_target_pairs={{0,8},{1,9},{2,10},{3,11},{4,12},{5,13},{6,14},{7,15},{16,24},{17,... | collective-permute-start | bytes 98312 | tf_op jit(solution)/shard_map/while/body/eval_jaxpr/ppermute | solution.py:35
  38.7 1.5 %collective-permute-done.2 = bf16[1,64,256]{2,1,0:T(8,128)(2,1)S(1)} collective-permute-done((bf16[1,64,256]{2,1,0:T(8,128)(2,1)S(1)}, bf16[1,64,256]{2,1,0:T(8,128)(2,1)S(1)}, u32[]{:S(2)}, u32[]{:S(2)}) %collective-permute-start.2) | collective-permute-done | bytes 32800 | tf_op jit(solution)/shard_map/while/body/eval_jaxpr/ppermute | solution.py:35
  40.3 0.6 bitcast_dynamic-update-slice_fusion.3
  40.9 0.6 copy-done.7
  41.6 1.9 %fusion.32 = f32[8,256,128]{1,2,0:T(8,128)S(1)} fusion(bf16[8,128,1,256]{3,1,0,2:T(8,128)(2,1)S(1)} %bitcast.136, bf16[8,128,1,256]{3,1,0,2:T(8,128)(2,1)S(1)} %bitcast.137, f32[8,128,256]{2,1,0:T(8,128)} %fusion.23), kind=kOutput, calls=%fused_computation.49 | convolution fusion | flops 136840448 | bytes 3145728 | tf_op jit(solution)/shard_map/nhqk,nkhd->nqhd/dot_general | solution.py:84
  43.5 0.3 copy.19
  43.8 3.2 %collective-permute-start.4 = (bf16[1,64,256]{2,1,0:T(8,128)(2,1)}, bf16[1,64,256]{2,1,0:T(8,128)(2,1)S(1)}, u32[]{:S(2)}, u32[]{:S(2)}) collective-permute-start(bf16[1,64,256]{2,1,0:T(8,128)(2,1)} %get-tuple-element.68), channel_id=1, source_target_pairs={{0,6},{2,0},{4,2},{6,4},{1,7},{3,1},{5,3},{7,5},{8,14},{10,8},{12,... | collective-permute-start | bytes 98312 | tf_op jit(solution)/shard_map/while/body/eval_jaxpr/ppermute | solution.py:25
  47.1 0.1 collective-permute-done.3
  47.2 0.8 bitcast_dynamic-update-slice_fusion.2
  48.0 1.0 %collective-permute-done.4 = bf16[1,64,256]{2,1,0:T(8,128)(2,1)S(1)} collective-permute-done((bf16[1,64,256]{2,1,0:T(8,128)(2,1)}, bf16[1,64,256]{2,1,0:T(8,128)(2,1)S(1)}, u32[]{:S(2)}, u32[]{:S(2)}) %collective-permute-start.4) | collective-permute-done | bytes 32800 | tf_op jit(solution)/shard_map/while/body/eval_jaxpr/ppermute | solution.py:25
  49.0 5.2 %reduce-scatter.5.cloned.1.call-done = bf16[1,2,64,256]{3,2,1,0:T(8,128)(2,1)} async-done(((bf16[1,2,256,256]{3,2,1,0:T(8,128)(2,1)}), bf16[1,2,64,256]{3,2,1,0:T(8,128)(2,1)}) %reduce-scatter.5.cloned.1.call-update) | async-done | bytes 65552 | tf_op jit(solution)/shard_map/while/body/eval_jaxpr/reduce_scatter | solution.py:123
  54.2 0.9 %multiply_reduce_fusion.3 = f32[2,64]{1,0:T(2,128)S(1)} fusion(bf16[1,2,64,256]{3,2,1,0:T(8,128)(2,1)} %reduce-scatter.5.cloned.1.call-done, bf16[1,2,256,256]{3,2,1,0:T(8,128)(2,1)S(1)} %copy-done.1, s32[]{:T(128)S(6)} %select_n.79), kind=kLoop, calls=%fused_computation.67 | loop fusion | flops 163712 | bytes 131588 | tf_op jit(solution)/shard_map/while/body/eval_jaxpr/reduce_sum | solution.py:48
  55.1 0.1 fusion.44
  55.2 0.9 %multiply_convert_fusion.3 = bf16[1,2,64,256]{3,2,1,0:T(8,128)(2,1)S(1)} fusion(bf16[1,2,64,256]{3,2,1,0:T(8,128)(2,1)} %reduce-scatter.5.cloned.1.call-done, f32[2,64]{1,0:T(2,128)S(1)} %fusion.44, bf16[1,2,256,256]{3,2,1,0:T(8,128)(2,1)S(1)} %copy-done.1, s32[]{:T(128)S(6)} %select_n.79), kind=kLoop, calls=%fused_computation.66 | loop fusion | flops 163840 | bytes 197124 | tf_op jit(solution)/shard_map/while/body/eval_jaxpr/convert_element_type | solution.py:49
  56.2 3.0 %collective-permute-start.6 = (bf16[1,2,64,256]{3,2,1,0:T(8,128)(2,1)S(1)}, bf16[1,2,64,256]{3,2,1,0:T(8,128)(2,1)S(1)}, u32[]{:S(2)}, u32[]{:S(2)}) collective-permute-start(bf16[1,2,64,256]{3,2,1,0:T(8,128)(2,1)S(1)} %multiply_convert_fusion.3), channel_id=1, source_target_pairs={{0,8},{1,9},{2,10},{3,11},{4,12},{5,13},{6,14},{7,15},{16,24},{17,... | collective-permute-start | bytes 196616 | tf_op jit(solution)/shard_map/while/body/eval_jaxpr/ppermute | solution.py:35
  59.2 1.9 %collective-permute-done.6 = bf16[1,2,64,256]{3,2,1,0:T(8,128)(2,1)S(1)} collective-permute-done((bf16[1,2,64,256]{3,2,1,0:T(8,128)(2,1)S(1)}, bf16[1,2,64,256]{3,2,1,0:T(8,128)(2,1)S(1)}, u32[]{:S(2)}, u32[]{:S(2)}) %collective-permute-start.6) | collective-permute-done | bytes 65568 | tf_op jit(solution)/shard_map/while/body/eval_jaxpr/ppermute | solution.py:35
  61.1 13.9 %all_gather.4 = bf16[1,2,256,256]{3,2,1,0:T(8,128)(2,1)S(1)} all-gather(bf16[1,2,64,256]{3,2,1,0:T(8,128)(2,1)S(1)} %broadcast_select_fusion), channel_id=1, replica_groups=mesh['groups'=2,'span'=2,'tok'=4,'head'=2] {'tok'}, dimensions={2}, use_global_device_ids=true | all-gather | bytes 327680 | tf_op jit(solution)/shard_map/while/body/eval_jaxpr/all_gather | solution.py:137
  75.0 1.3 %convolution_bitcast_fusion.7 = f32[1024,1,256]{0,2,1:T(8,128)} fusion(bf16[1024,1,256]{2,0,1:T(8,128)(2,1)S(1)} %fusion.27, bf16[1,2,256,256]{3,2,1,0:T(8,128)(2,1)S(1)} %all_gather.4), kind=kOutput, calls=%fused_computation.31 | convolution fusion | flops 134217728 | bytes 1703936 | tf_op jit(solution)/shard_map/thd,hfd->thf/dot_general | solution.py:146
  76.3 1.9 %multiply_reduce_fusion = (f32[1024]{0:T(1024)S(1)}, f32[1,256,1024]{2,1,0:T(8,128)S(1)}) fusion(bf16[256,256]{1,0:T(8,128)(2,1)S(1)} %bitcast_dynamic-update-slice_fusion, f32[1024,1,256]{0,2,1:T(8,128)} %convolution_bitcast_fusion.7, bf16[1024,1,256]{2,0,1:T(8,128)(2,1)S(1)} %fusion.27, bf16[1,2,256,256]{3,2,1,0:T(8,128)(2,1)S(1)} %all_gather.4), kind=kOutput, calls=%fused_computation.54 | convolution fusion | flops 270531584 | bytes 2887680 | tf_op jit(solution)/shard_map/thf,hdf->thd/dot_general | solution.py:153
  78.2 0.2 fusion.35
  78.4 1.0 %copy.20 = bf16[1024,1,256]{2,0,1:T(8,128)(2,1)} copy(bf16[1024,1,256]{0,2,1:T(8,128)(2,1)S(1)} %fusion.35) | data formatting | bytes 1048576 | tf_op jit(solution)/shard_map/convert_element_type | solution.py:170
  (42 shorter events, 0.3 us)
Async XLA Ops:
  6.5 2.7 %copy-start.3 = (bf16[1024,1,256]{2,0,1:T(8,128)(2,1)S(1)}, bf16[1024,1,256]{2,0,1:T(8,128)(2,1)}, u32[]{:S(2)}) copy-start(bf16[1024,1,256]{2,0,1:T(8,128)(2,1)} %param.12) | copy-start | bytes 1572868
  6.5 2.7 %copy-start.10 = (f32[1024,1]{0,1:T(1,128)S(1)}, f32[1024,1]{0,1:T(1,128)}, u32[]{:S(2)}) copy-start(f32[1024,1]{0,1:T(1,128)} %param.13) | copy-start | bytes 12292
  6.5 2.7 %copy-start.1 = (bf16[1,2,256,256]{3,2,1,0:T(8,128)(2,1)S(1)}, bf16[1,2,256,256]{3,2,1,0:T(8,128)(2,1)}, u32[]{:S(2)}) copy-start(bf16[1,2,256,256]{3,2,1,0:T(8,128)(2,1)} %param.14) | copy-start | bytes 786436
  6.5 2.7 %copy-start.6 = (bf16[1,256,256]{2,1,0:T(8,128)(2,1)S(1)}, bf16[1,256,256]{2,1,0:T(8,128)(2,1)}, u32[]{:S(2)}) copy-start(bf16[1,256,256]{2,1,0:T(8,128)(2,1)} %param.15) | copy-start | bytes 393220
  6.5 27.0 %reduce-scatter.3.cloned.1.call-start = ((), (), s32[]{:S(2)}) async-start(), calls=%async_computation.2 | async-start | bytes 163840 | tf_op jit(solution)/shard_map/while/body/eval_jaxpr/reduce_scatter | solution.py:126
  11.8 0.6 copy-start.5
  11.8 9.2 %copy-start.2 = (bf16[1,2,256,256]{3,2,1,0:T(8,128)(2,1)}, bf16[1,2,256,256]{3,2,1,0:T(8,128)(2,1)S(1)}, u32[]{:S(2)}) copy-start(bf16[1,2,256,256]{3,2,1,0:T(8,128)(2,1)S(1)} %get-tuple-element.45) | copy-start | bytes 786436
  12.5 41.7 %reduce-scatter.5.cloned.1.call-start = ((), (), s32[]{:S(2)}) async-start(), calls=%async_computation.3 | async-start | bytes 327680 | tf_op jit(solution)/shard_map/while/body/eval_jaxpr/reduce_scatter | solution.py:123
  12.5 10.4 %collective-permute-start.1 = (bf16[128,1,256]{2,0,1:T(8,128)(2,1)S(1)}, bf16[128,1,256]{2,0,1:T(8,128)(2,1)S(1)}, u32[]{:S(2)}, u32[]{:S(2)}) collective-permute-start(bf16[128,1,256]{2,0,1:T(8,128)(2,1)S(1)} %slice.30), channel_id=1, source_target_pairs={{0,2},{2,4},{4,6},{6,8},{8,10},{10,12},{12,14},{1,3},{3,5},{5,7},{... | collective-permute-start | bytes 196616 | tf_op jit(solution)/shard_map/ppermute | solution.py:35
  17.5 21.2 %collective-permute-start = (bf16[128,1,256]{2,0,1:T(8,128)(2,1)S(1)}, bf16[128,1,256]{2,0,1:T(8,128)(2,1)S(1)}, u32[]{:S(2)}, u32[]{:S(2)}) collective-permute-start(bf16[128,1,256]{2,0,1:T(8,128)(2,1)S(1)} %slice.24), channel_id=1, source_target_pairs={{0,2},{2,4},{4,6},{6,8},{8,10},{10,12},{12,14},{1,3},{3,5},{5,7},{... | collective-permute-start | bytes 196616 | tf_op jit(solution)/shard_map/ppermute | solution.py:35
  21.2 1.0 %copy-start = (bf16[1024,1,256]{2,0,1:T(8,128)(2,1)S(1)}, bf16[1024,1,256]{2,0,1:T(8,128)(2,1)}, u32[]{:S(2)}) copy-start(bf16[1024,1,256]{2,0,1:T(8,128)(2,1)} %param.10) | copy-start | bytes 1572868
  21.5 1.3 %copy-start.11 = (s32[64]{0:T(128)S(1)}, s32[64]{0:T(128)}, u32[]{:S(2)}) copy-start(s32[64]{0:T(128)} %param.17) | copy-start | bytes 772
  24.4 17.1 %copy-start.4 = (bf16[1024,1,256]{2,0,1:T(8,128)(2,1)S(1)}, bf16[1024,1,256]{2,0,1:T(8,128)(2,1)}, u32[]{:S(2)}) copy-start(bf16[1024,1,256]{2,0,1:T(8,128)(2,1)} %param.12) | copy-start | bytes 1572868
  35.4 4.9 %collective-permute-start.2 = (bf16[1,64,256]{2,1,0:T(8,128)(2,1)S(1)}, bf16[1,64,256]{2,1,0:T(8,128)(2,1)S(1)}, u32[]{:S(2)}, u32[]{:S(2)}) collective-permute-start(bf16[1,64,256]{2,1,0:T(8,128)(2,1)S(1)} %multiply_convert_fusion.4), channel_id=1, source_target_pairs={{0,8},{1,9},{2,10},{3,11},{4,12},{5,13},{6,14},{7,15},{16,24},{17,... | collective-permute-start | bytes 98312 | tf_op jit(solution)/shard_map/while/body/eval_jaxpr/ppermute | solution.py:35
  40.9 0.6 copy-start.7
  40.9 6.3 %collective-permute-start.3 = (bf16[1,64,256]{2,1,0:T(8,128)(2,1)}, bf16[1,64,256]{2,1,0:T(8,128)(2,1)}, u32[]{:S(2)}, u32[]{:S(2)}) collective-permute-start(bf16[1,64,256]{2,1,0:T(8,128)(2,1)} %get-tuple-element.68), channel_id=1, source_target_pairs={{0,2},{2,4},{4,6},{6,0},{1,3},{3,5},{5,7},{7,1},{8,10},{10,12},{12... | collective-permute-start | bytes 98312 | tf_op jit(solution)/shard_map/while/body/eval_jaxpr/ppermute | solution.py:20
  43.5 3.7 %copy-start.8 = (bf16[256,256]{1,0:T(8,128)(2,1)S(1)}, bf16[256,256]{1,0:T(8,128)(2,1)}, u32[]{:S(2)}) copy-start(bf16[256,256]{1,0:T(8,128)(2,1)} %copy-done.7) | copy-start | bytes 393220
  43.8 5.2 %collective-permute-start.4 = (bf16[1,64,256]{2,1,0:T(8,128)(2,1)}, bf16[1,64,256]{2,1,0:T(8,128)(2,1)S(1)}, u32[]{:S(2)}, u32[]{:S(2)}) collective-permute-start(bf16[1,64,256]{2,1,0:T(8,128)(2,1)} %get-tuple-element.68), channel_id=1, source_target_pairs={{0,6},{2,0},{4,2},{6,4},{1,7},{3,1},{5,3},{7,5},{8,14},{10,8},{12,... | collective-permute-start | bytes 98312 | tf_op jit(solution)/shard_map/while/body/eval_jaxpr/ppermute | solution.py:25
  47.2 12.0 %collective-permute-start.5 = (bf16[1,64,256]{2,1,0:T(8,128)(2,1)}, bf16[1,64,256]{2,1,0:T(8,128)(2,1)S(1)}, u32[]{:S(2)}, u32[]{:S(2)}) collective-permute-start(bf16[1,64,256]{2,1,0:T(8,128)(2,1)} %collective-permute-done.3), channel_id=1, source_target_pairs={{0,2},{2,4},{4,6},{6,0},{1,3},{3,5},{5,7},{7,1},{8,10},{10,12},{12... | collective-permute-start | bytes 98312 | tf_op jit(solution)/shard_map/while/body/eval_jaxpr/ppermute | solution.py:20
  56.2 4.9 %collective-permute-start.6 = (bf16[1,2,64,256]{3,2,1,0:T(8,128)(2,1)S(1)}, bf16[1,2,64,256]{3,2,1,0:T(8,128)(2,1)S(1)}, u32[]{:S(2)}, u32[]{:S(2)}) collective-permute-start(bf16[1,2,64,256]{3,2,1,0:T(8,128)(2,1)S(1)} %multiply_convert_fusion.3), channel_id=1, source_target_pairs={{0,8},{1,9},{2,10},{3,11},{4,12},{5,13},{6,14},{7,15},{16,24},{17,... | collective-permute-start | bytes 196616 | tf_op jit(solution)/shard_map/while/body/eval_jaxpr/ppermute | solution.py:35
  76.3 1.9 %copy-start.9 = (f32[1,256]{1,0:T(1,128)S(1)}, f32[1,256]{1,0:T(1,128)}, u32[]{:S(2)}) copy-start(f32[1,256]{1,0:T(1,128)} %param.16) | copy-start | bytes 3076
Sparse Core Ops, SparseCore 0:
  12.6 20.9 reduce-scatter.2
  35.9 18.2 reduce-scatter.4
